TPU v7x, 32 devices: a whole 2x2x4 slice. The times are simulated.
32 devices in a mesh: groups: 2 (over x), tok: 4 (over y, core), hid: 4 (over z).
Axes of the slice: x: 2, y: 2, z: 4, core: 2. Of those that a mesh axis runs over, the one named last changes fastest.
Arguments:
- tokens: bfloat16 [2048, 5376], P(('groups', 'tok'), 'hid'), parts along dimension 0, may hold values from -6 to 6
- w_query: bfloat16 [5376, 2048], P('tok', 'hid'), may hold values from -0.078125 to 0.078125
- key_weight: bfloat16 [5376, 1024], P('tok', 'hid'), may hold values from -0.078125 to 0.078125
- value_weight: bfloat16 [5376, 1024], P('tok', 'hid'), may hold values from -0.078125 to 0.078125
- w_out: bfloat16 [2048, 5376], P('tok', 'hid'), may hold values from -0.5 to 0.5
- query_norm_gain: float32 [128], replicated, may hold values from 0.5 to 2
- key_gain: float32 [128], replicated, may hold values from 0.5 to 2
- positions: int32 [2048], P('groups'), parts along dimension 0, may hold values from 0 to 131071, as said below
- grad_out: bfloat16 [2048, 5376], P(('groups', 'tok'), 'hid'), parts along dimension 0, may hold values from -6 to 6
Outputs:
- attn_out: bfloat16 [2048, 5376], P(('groups', 'tok'), 'hid'), parts along dimension 0
- grad_x: bfloat16 [2048, 5376], P(('groups', 'tok'), 'hid'), parts along dimension 0
- grad_wq: float32 [10752, 2048], P(('groups', 'tok'), 'hid'), parts along dimension 0
- key_weight_gradient: float32 [10752, 1024], P(('groups', 'tok'), 'hid'), parts along dimension 0
- value_weight_gradient: float32 [10752, 1024], P(('groups', 'tok'), 'hid'), parts along dimension 0
- grad_wo: float32 [4096, 5376], P(('groups', 'tok'), 'hid'), parts along dimension 0
There are 2 independent parts, one for each index of `groups`. A program takes and returns all parts, laid end to end along the dimension named above; an argument that names none is the same for every part. Nothing has to cross between parts.
Inputs may be any that keep to these rules, and one draw needn't show every extreme that they name: positions[t] is token t's position in its document: it rises by one from token to token and is 0 where a document begins; the first document begins before the window and its last token in the window has position 131071; at least one document begins inside the window.
All inputs are finite; a program needn't handle non-finite values.
Results may differ from a plain program's by a relative error of at most 0.02.
Values may be sent and summed in bfloat16 or wider, within the bound.
A program may use at most 192 MiB of HBM per device.

v0:
```python
import jax
import jax.numpy as jnp
from jax import lax
from jax.sharding import PartitionSpec as P

QUERY_HEADS = 16
KEY_VALUE_HEADS = 8
HEAD_SIZE = 128
WINDOW = 1024
TOK_DEV = 256
attn_scale = 168.0 ** (-0.5)
rope_base = 10000.0
norm_eps = 1e-06


def from_behind(value, axis, steps):
    count = lax.axis_size(axis)
    first, last = (max(0, -steps), min(count, count - steps))
    return lax.ppermute(value, axis, [(source, source + steps) for source in range(first, last)])


def rotary_tables(token_pos):
    half_dim = HEAD_SIZE // 2
    freqs = rope_base ** (-jnp.arange(half_dim, dtype=jnp.float32) * 2.0 / HEAD_SIZE)
    angles = token_pos.astype(jnp.float32)[:, None] * freqs[None, :]
    return (jnp.cos(angles), jnp.sin(angles))


def prepare_inputs(raw_values, gain_vector, cosine_table, sine_table):
    scaled = (
        raw_values
        * lax.rsqrt(jnp.mean(raw_values * raw_values, -1, keepdims=True) + norm_eps)
        * gain_vector
    )
    half_dim = scaled.shape[-1] // 2
    first_half = scaled[..., :half_dim]
    second_half = scaled[..., half_dim:]
    cos_rows = cosine_table[:, None, :]
    sin_rows = sine_table[:, None, :]
    return jnp.concatenate(
        [
            first_half * cos_rows - second_half * sin_rows,
            second_half * cos_rows + first_half * sin_rows,
        ],
        -1,
    )


def local(
    tokens, w_query, key_weight, value_weight, w_out, query_norm_gain, key_gain, positions, grad_out
):
    hidden_count = lax.axis_size("hid")
    block_index = lax.axis_index("tok")
    query_heads = QUERY_HEADS // hidden_count
    key_value_heads = KEY_VALUE_HEADS // hidden_count
    group_width = QUERY_HEADS // KEY_VALUE_HEADS
    reach = WINDOW // TOK_DEV
    span_rows = (reach + 1) * TOK_DEV
    leading_part = reach * TOK_DEV
    first_token = block_index * TOK_DEV
    query_cols = query_heads * HEAD_SIZE
    kv_cols = key_value_heads * HEAD_SIZE
    full_rows = lax.all_gather(tokens, "hid", axis=1, tiled=True)
    pieces = (
        lax.all_gather(w_query, "tok", axis=0, tiled=True),
        lax.all_gather(key_weight, "tok", axis=0, tiled=True),
        lax.all_gather(value_weight, "tok", axis=0, tiled=True),
    )
    columns = full_rows
    query_unnormed = jnp.dot(columns, pieces[0], preferred_element_type=jnp.float32)
    key_unnormed = jnp.dot(columns, pieces[1], preferred_element_type=jnp.float32)
    value_raw = jnp.dot(columns, pieces[2], preferred_element_type=jnp.float32)
    values_local = value_raw.astype(jnp.bfloat16)
    token_pos = lax.dynamic_slice_in_dim(positions, first_token, TOK_DEV, 0)
    cosine_table, sine_table = rotary_tables(token_pos)
    query_heads_raw = query_unnormed.reshape(TOK_DEV, query_heads, HEAD_SIZE)
    key_heads_raw = key_unnormed.reshape(TOK_DEV, key_value_heads, HEAD_SIZE)
    query_rows = (
        prepare_inputs(query_heads_raw, query_norm_gain, cosine_table, sine_table)
        .astype(jnp.bfloat16)
        .reshape(TOK_DEV, key_value_heads, group_width, HEAD_SIZE)
    )
    keys_local = prepare_inputs(key_heads_raw, key_gain, cosine_table, sine_table).astype(
        jnp.bfloat16
    )
    key_value = jnp.stack([keys_local.reshape(TOK_DEV, kv_cols), values_local], 0)
    blocks = [key_value]
    moving = key_value
    for turn_index in range(reach):
        moving = from_behind(moving, "tok", 1)
        blocks = [moving] + blocks
    window = jnp.concatenate(blocks, 1)
    key_window = window[0].reshape(span_rows, key_value_heads, HEAD_SIZE)
    value_window = window[1].reshape(span_rows, key_value_heads, HEAD_SIZE)
    query_index = first_token + jnp.arange(TOK_DEV, dtype=jnp.int32)
    key_index = first_token - leading_part + jnp.arange(span_rows, dtype=jnp.int32)
    padded_pos = jnp.pad(positions, (leading_part, 0))
    key_pos = lax.dynamic_slice_in_dim(padded_pos, first_token, span_rows, 0)
    distance = query_index[:, None] - key_index[None, :]
    allowed = (
        (key_index[None, :] >= 0)
        & (distance >= 0)
        & (distance < WINDOW)
        & (token_pos[:, None] - key_pos[None, :] == distance)
    )
    scores = (
        jnp.einsum("tkgd,ukd->kgtu", query_rows, key_window, preferred_element_type=jnp.float32)
        * attn_scale
    )
    weights = jnp.where(allowed[None, None], jnp.exp(scores), 0.0)
    probabilities = weights / jnp.sum(weights, -1, keepdims=True)
    rounded = probabilities.astype(jnp.bfloat16)
    attended = jnp.einsum(
        "kgtu,ukd->tkgd", rounded, value_window, preferred_element_type=jnp.float32
    )
    attended = attended.astype(jnp.bfloat16).reshape(TOK_DEV, query_cols)
    all_heads = lax.all_gather(attended, "hid", axis=1, tiled=True)
    columns = all_heads
    output = jnp.dot(
        columns,
        lax.all_gather(w_out, "tok", axis=0, tiled=True),
        preferred_element_type=jnp.float32,
    )
    attn_out = output.astype(jnp.bfloat16)
    partial_heads = jnp.einsum(
        "td,hd->th",
        grad_out,
        lax.all_gather(w_out, "tok", axis=0, tiled=True),
        preferred_element_type=jnp.float32,
    )
    attended_gradient = lax.psum_scatter(
        partial_heads.astype(jnp.bfloat16), "hid", scatter_dimension=1, tiled=True
    )
    attended_gradient = attended_gradient.reshape(TOK_DEV, key_value_heads, group_width, HEAD_SIZE)
    columns = all_heads
    grad_wo = lax.psum_scatter(
        jnp.einsum("th,td->hd", columns, grad_out, preferred_element_type=jnp.float32).astype(
            jnp.bfloat16
        ),
        "tok",
        scatter_dimension=0,
        tiled=True,
    ).astype(jnp.float32)
    grad_probs = jnp.einsum(
        "tkgd,ukd->kgtu", attended_gradient, value_window, preferred_element_type=jnp.float32
    )
    grad_scores = (
        attn_scale
        * probabilities
        * (grad_probs - jnp.sum(probabilities * grad_probs, -1, keepdims=True))
    )
    grad_scores = grad_scores.astype(jnp.bfloat16)
    grad_queries = jnp.einsum(
        "kgtu,ukd->tkgd", grad_scores, key_window, preferred_element_type=jnp.float32
    )
    keys_gradient = jnp.einsum(
        "kgtu,tkgd->ukd", grad_scores, query_rows, preferred_element_type=jnp.float32
    )
    values_gradient = jnp.einsum(
        "kgtu,tkgd->ukd", rounded, attended_gradient, preferred_element_type=jnp.float32
    )
    grad_window = jnp.stack(
        [keys_gradient.reshape(span_rows, kv_cols), values_gradient.reshape(span_rows, kv_cols)], 0
    )
    grad_kv = grad_window[:, :TOK_DEV]
    for turn_index in range(1, reach + 1):
        grad_kv = (
            from_behind(grad_kv.astype(jnp.bfloat16), "tok", -1).astype(grad_kv.dtype)
            + grad_window[:, turn_index * TOK_DEV : (turn_index + 1) * TOK_DEV]
        )
    _, query_pull = jax.vjp(
        lambda raw_values: prepare_inputs(raw_values, query_norm_gain, cosine_table, sine_table),
        query_heads_raw,
    )
    _, key_pullback = jax.vjp(
        lambda raw_values: prepare_inputs(raw_values, key_gain, cosine_table, sine_table),
        key_heads_raw,
    )
    query_back = (
        query_pull(grad_queries.reshape(TOK_DEV, query_heads, HEAD_SIZE))[0]
        .astype(jnp.bfloat16)
        .reshape(TOK_DEV, query_cols)
    )
    key_backward = (
        key_pullback(grad_kv[0].reshape(TOK_DEV, key_value_heads, HEAD_SIZE))[0]
        .astype(jnp.bfloat16)
        .reshape(TOK_DEV, kv_cols)
    )
    value_backward = grad_kv[1].astype(jnp.bfloat16)
    pieces = (
        lax.all_gather(w_query, "tok", axis=0, tiled=True),
        lax.all_gather(key_weight, "tok", axis=0, tiled=True),
        lax.all_gather(value_weight, "tok", axis=0, tiled=True),
    )
    block_rows = jnp.einsum("tc,dc->td", query_back, pieces[0], preferred_element_type=jnp.float32)
    block_rows = block_rows + jnp.einsum(
        "tc,dc->td", key_backward, pieces[1], preferred_element_type=jnp.float32
    )
    block_rows = block_rows + jnp.einsum(
        "tc,dc->td", value_backward, pieces[2], preferred_element_type=jnp.float32
    )
    grad_x = lax.psum_scatter(
        block_rows.astype(jnp.bfloat16), "hid", scatter_dimension=1, tiled=True
    )
    joined = jnp.concatenate([query_back, key_backward, value_backward], 1)
    columns = full_rows
    inputs_gradient = lax.psum_scatter(
        jnp.einsum("td,tc->dc", columns, joined, preferred_element_type=jnp.float32).astype(
            jnp.bfloat16
        ),
        "tok",
        scatter_dimension=0,
        tiled=True,
    ).astype(jnp.float32)
    grad_wq = inputs_gradient[:, :query_cols]
    key_weight_gradient = inputs_gradient[:, query_cols : query_cols + kv_cols]
    value_weight_gradient = inputs_gradient[:, query_cols + kv_cols :]
    return (attn_out, grad_x, grad_wq, key_weight_gradient, value_weight_gradient, grad_wo)


def solution(mesh):
    return jax.shard_map(
        local,
        mesh=mesh,
        in_specs=(
            P(("groups", "tok"), "hid"),
            P("tok", "hid"),
            P("tok", "hid"),
            P("tok", "hid"),
            P("tok", "hid"),
            P(),
            P(),
            P("groups"),
            P(("groups", "tok"), "hid"),
        ),
        out_specs=(
            P(("groups", "tok"), "hid"),
            P(("groups", "tok"), "hid"),
            P(("groups", "tok"), "hid"),
            P(("groups", "tok"), "hid"),
            P(("groups", "tok"), "hid"),
            P(("groups", "tok"), "hid"),
        ),
        check_vma=False,
    )
```

profile of v0, /device:TPU:0, one launch (start us, length us, event | category | flops | bytes accessed | tf_op | source)
XLA Modules:
  0.0 533.1 jit_solution(8596791121754949615)
XLA Ops:
  12.1 57.2 %all-gather.7.cloned.1.call-done = bf16[256,5376]{0,1:T(8,128)(2,1)} async-done(((bf16[256,1344]{0,1:T(8,128)(2,1)}), bf16[256,5376]{0,1:T(8,128)(2,1)}) %all-gather.7.cloned.1.call-update) | async-done | bytes 2752528 | tf_op jit(solution)/shard_map/all_gather | solution.py:63
  69.3 26.6 %all-gather.9.cloned.1.call-done = bf16[5376,256]{1,0:T(8,128)(2,1)} async-done(((bf16[1344,256]{1,0:T(8,128)(2,1)}), bf16[5376,256]{1,0:T(8,128)(2,1)}) %all-gather.9.cloned.1.call-update) | async-done | bytes 2752528 | tf_op jit(solution)/shard_map/all_gather | solution.py:66
  95.9 3.8 multiply_reduce_fusion.3
  103.0 20.9 %all-gather.11.cloned.1.call-done = bf16[5376,256]{1,0:T(8,128)(2,1)} async-done(((bf16[1344,256]{1,0:T(8,128)(2,1)}), bf16[5376,256]{1,0:T(8,128)(2,1)}) %all-gather.11.cloned.1.call-update) | async-done | bytes 2752528 | tf_op jit(solution)/shard_map/all_gather | solution.py:67
  123.9 2.7 fusion.17
  127.3 2.1 collective-permute-start
  131.3 4.9 collective-permute-start.1
  137.0 12.5 %collective-permute-start.2 = (bf16[2,256,256]{2,1,0:T(8,128)(2,1)}, bf16[2,256,256]{2,1,0:T(8,128)(2,1)}, u32[]{:S(2)}, u32[]{:S(2)}) collective-permute-start(bf16[2,256,256]{2,1,0:T(8,128)(2,1)} %collective-permute-done.1), channel_id=1, source_target_pairs={{0,4},{4,8},{8,12},{1,5},{5,9},{9,13},{2,6},{6,10},{10,14},{3,7},{... | collective-permute-start | bytes 786440 | tf_op jit(solution)/shard_map/ppermute | solution.py:19
  150.3 12.2 %collective-permute-start.3 = (bf16[2,256,256]{2,1,0:T(8,128)(2,1)}, bf16[2,256,256]{2,1,0:T(8,128)(2,1)S(1)}, u32[]{:S(2)}, u32[]{:S(2)}) collective-permute-start(bf16[2,256,256]{2,1,0:T(8,128)(2,1)} %collective-permute-done.2), channel_id=1, source_target_pairs={{0,4},{4,8},{8,12},{1,5},{5,9},{9,13},{2,6},{6,10},{10,14},{3,7},{... | collective-permute-start | bytes 786440 | tf_op jit(solution)/shard_map/ppermute | solution.py:19
  162.5 2.1 fusion.11
  165.3 1.7 constant_dynamic-update-slice_fusion.3
  167.0 1.7 constant_dynamic-update-slice_fusion.2
  170.9 5.3 %convolution_convert_fusion.3 = bf16[256,2048]{1,0:T(8,128)(2,1)} fusion(bf16[256,1344]{0,1:T(8,128)(2,1)S(1)} %copy-done, bf16[2048,1344]{0,1:T(8,128)(2,1)} %all-gather.17.cloned.1.call-done), kind=kOutput, calls=%fused_computation.23 | convolution fusion | flops 1409810432 | bytes 7241728 | tf_op jit(solution)/shard_map/td,hd->th/dot_general | solution.py:125
  176.5 1.7 constant_dynamic-update-slice_fusion
  178.2 2.4 fusion.50
  180.6 2.5 reshape_squeeze.9
  183.2 2.6 reshape_squeeze.10
  185.7 3.0 copy.117
  188.7 29.4 %all-gather.13.cloned.1.call-done = bf16[5376,512]{1,0:T(8,128)(2,1)} async-done(((bf16[1344,512]{1,0:T(8,128)(2,1)}), bf16[5376,512]{1,0:T(8,128)(2,1)}) %all-gather.13.cloned.1.call-update) | async-done | bytes 5505040 | tf_op jit(solution)/shard_map/all_gather | solution.py:65
  218.1 5.0 fusion.53
  225.9 22.1 %reduce-scatter.7.cloned.1.call-done = bf16[256,512]{1,0:T(8,128)(2,1)} async-done(((bf16[256,2048]{1,0:T(8,128)(2,1)}), bf16[256,512]{1,0:T(8,128)(2,1)}) %reduce-scatter.7.cloned.1.call-update) | async-done | bytes 262160 | tf_op jit(solution)/shard_map/reduce_scatter | solution.py:131
  249.1 3.2 fusion.19
  252.3 7.2 %fusion.2 = (f32[2,2,256]{2,1,0:T(2,128)S(1)}, f32[2,2,256,1280]{2,3,1,0:T(8,128)}) fusion(f32[2,1280,256,2]{2,1,3,0:T(8,128)} %fusion.19, bf16[1280,2,128,1]{0,2,3,1:T(8,128)(2,1)S(1)} %copy-done.14, pred[256,1280]{0,1:T(8,128)(4,1)S(1)} %copy-done.34, bf16[256,2,2,64]{3,0,2,1:T(8,128)(2,1)S(1)} %bitcast.103, bf16[256,2,2,64]{3,0,2,1:T(8,128)(2,1)S(1)} %bitcast.105), kind=kOutput, calls=%fused_computation.8 | convolution fusion | flops 342623488 | bytes 11735040 | tf_op jit(solution)/shard_map/div | solution.py:111
  259.5 3.8 fusion.14
  263.3 26.7 %all-gather.15.cloned.1.call-done = bf16[256,2048]{0,1:T(8,128)(2,1)} async-done(((bf16[256,512]{0,1:T(8,128)(2,1)}), bf16[256,2048]{0,1:T(8,128)(2,1)}) %all-gather.15.cloned.1.call-update) | async-done | bytes 1048592 | tf_op jit(solution)/shard_map/all_gather | solution.py:117
  290.0 5.2 convolution_convert_fusion.1
  295.5 4.8 fusion.4
  301.4 4.5 fusion.7
  307.5 2.1 collective-permute-done.4
  314.2 3.2 collective-permute-done.5
  317.4 1.7 fusion.32
  322.5 10.5 %collective-permute-done.6 = bf16[2,256,256]{1,2,0:T(8,128)(2,1)} collective-permute-done((bf16[2,256,256]{1,2,0:T(8,128)(2,1)}, bf16[2,256,256]{1,2,0:T(8,128)(2,1)}, u32[]{:S(2)}, u32[]{:S(2)}) %collective-permute-start.6) | collective-permute-done | bytes 262176 | tf_op jit(solution)/shard_map/ppermute | solution.py:19
  333.0 1.7 fusion.24
  336.2 2.0 fusion.21
  339.0 9.6 %collective-permute-done.7 = bf16[2,256,256]{1,2,0:T(8,128)(2,1)} collective-permute-done((bf16[2,256,256]{1,2,0:T(8,128)(2,1)}, bf16[2,256,256]{1,2,0:T(8,128)(2,1)}, u32[]{:S(2)}, u32[]{:S(2)}) %collective-permute-start.7) | collective-permute-done | bytes 262176 | tf_op jit(solution)/shard_map/ppermute | solution.py:19
  352.2 7.7 %fusion = bf16[5376,1024]{0,1:T(8,128)(2,1)} fusion(bf16[256,5376]{0,1:T(8,128)(2,1)} %all-gather.7.cloned.1.call-done, bf16[256,256]{1,0:T(8,128)(2,1)S(1)} %copy.109, bf16[256,256]{1,0:T(8,128)(2,1)S(1)} %copy.108, bf16[256,512]{1,0:T(8,128)(2,1)S(1)} %bitcast.102), kind=kOutput, calls=%fused_computation.1 | convolution fusion | flops 2825650176 | bytes 14286848 | tf_op jit(solution)/shard_map/td,tc->dc/dot_general | solution.py:208
  359.9 14.7 %copy.133 = bf16[5376,1024]{1,0:T(8,128)(2,1)} copy(bf16[5376,1024]{0,1:T(8,128)(2,1)} %fusion) | data formatting | bytes 22020096
  375.5 4.3 fusion.47
  381.7 2.5 fusion.1
  385.5 5.5 %convolution_convert_fusion.2 = bf16[256,1344]{0,1:T(8,128)(2,1)} fusion(bf16[2048,1344]{0,1:T(8,128)(2,1)} %all-gather.17.cloned.1.call-done, bf16[256,2048]{0,1:T(8,128)(2,1)S(1)} %copy-done.26), kind=kOutput, calls=%fused_computation.22 | convolution fusion | flops 1409630208 | bytes 7241728 | tf_op jit(solution)/shard_map/dot_general | solution.py:119
  391.0 3.6 convert_element_type.111
  394.6 74.7 %reduce-scatter.13.cloned.1.call-done = bf16[1344,1024]{1,0:T(8,128)(2,1)} async-done(((bf16[5376,1024]{1,0:T(8,128)(2,1)}), bf16[1344,1024]{1,0:T(8,128)(2,1)}) %reduce-scatter.13.cloned.1.call-update) | async-done | bytes 2752528
  469.3 4.6 copy.134
  473.9 3.1 slice.82
  477.0 3.8 copy.110
  480.8 2.6 fusion.49
  483.4 2.9 copy.111
  487.8 38.4 %reduce-scatter.9.cloned.1.call-done = bf16[256,1344]{0,1:T(8,128)(2,1)} async-done(((bf16[256,5376]{0,1:T(8,128)(2,1)}), bf16[256,1344]{0,1:T(8,128)(2,1)}) %reduce-scatter.9.cloned.1.call-update) | async-done | bytes 688144 | tf_op jit(solution)/shard_map/reduce_scatter | solution.py:202
  (157 shorter events, 41.0 us)
Async XLA Ops:
  7.2 163.8 %copy-start = (bf16[256,1344]{0,1:T(8,128)(2,1)S(1)}, bf16[256,1344]{0,1:T(8,128)(2,1)}, u32[]{:S(2)}) copy-start(bf16[256,1344]{0,1:T(8,128)(2,1)} %param.17) | copy-start | bytes 2064388
  7.2 3.5 copy-start.36
  7.2 62.1 %all-gather.7.cloned.1.call-start = ((), (), s32[]{:S(2)}) async-start(), calls=%async_computation.4 | async-start | bytes 3440640 | tf_op jit(solution)/shard_map/all_gather | solution.py:63
  7.9 88.0 %all-gather.9.cloned.1.call-start = ((), (), s32[]{:S(2)}) async-start(), calls=%async_computation.5 | async-start | bytes 3440640 | tf_op jit(solution)/shard_map/all_gather | solution.py:66
  8.7 115.2 %all-gather.11.cloned.1.call-start = ((), (), s32[]{:S(2)}) async-start(), calls=%async_computation.6 | async-start | bytes 3440640 | tf_op jit(solution)/shard_map/all_gather | solution.py:67
  9.4 161.5 %all-gather.17.cloned.1.call-start = ((), (), s32[]{:S(2)}) async-start(), calls=%async_computation.9 | async-start | bytes 6881280 | tf_op jit(solution)/shard_map/all_gather | solution.py:121
  10.0 208.1 %all-gather.13.cloned.1.call-start = ((), (), s32[]{:S(2)}) async-start(), calls=%async_computation.7 | async-start | bytes 6881280 | tf_op jit(solution)/shard_map/all_gather | solution.py:65
  10.6 237.4 %reduce-scatter.7.cloned.1.call-start = ((), (), s32[]{:S(2)}) async-start(), calls=%async_computation.10 | async-start | bytes 1310720 | tf_op jit(solution)/shard_map/reduce_scatter | solution.py:131
  12.1 88.4 %copy-start.38 = (f32[128]{0:T(128)S(1)}, f32[128]{0:T(128)}, u32[]{:S(2)}) copy-start(f32[128]{0:T(128)} %param.15) | copy-start | bytes 1540
  69.3 54.6 %copy-start.2 = (bf16[256,5376]{0,1:T(8,128)(2,1)S(1)}, bf16[256,5376]{0,1:T(8,128)(2,1)}, u32[]{:S(2)}) copy-start(bf16[256,5376]{0,1:T(8,128)(2,1)} %all-gather.7.cloned.1.call-done) | copy-start | bytes 8257540
  95.9 4.6 copy-start.31
  123.9 2.8 copy-start.29
  127.3 3.3 collective-permute-start
  131.3 5.8 %collective-permute-start.1 = (bf16[2,256,256]{2,1,0:T(8,128)(2,1)S(1)}, bf16[2,256,256]{2,1,0:T(8,128)(2,1)}, u32[]{:S(2)}, u32[]{:S(2)}) collective-permute-start(bf16[2,256,256]{2,1,0:T(8,128)(2,1)S(1)} %collective-permute-done), channel_id=1, source_target_pairs={{0,4},{4,8},{8,12},{1,5},{5,9},{9,13},{2,6},{6,10},{10,14},{3,7},{... | collective-permute-start | bytes 786440 | tf_op jit(solution)/shard_map/ppermute | solution.py:19
  137.0 13.2 %collective-permute-start.2 = (bf16[2,256,256]{2,1,0:T(8,128)(2,1)}, bf16[2,256,256]{2,1,0:T(8,128)(2,1)}, u32[]{:S(2)}, u32[]{:S(2)}) collective-permute-start(bf16[2,256,256]{2,1,0:T(8,128)(2,1)} %collective-permute-done.1), channel_id=1, source_target_pairs={{0,4},{4,8},{8,12},{1,5},{5,9},{9,13},{2,6},{6,10},{10,14},{3,7},{... | collective-permute-start | bytes 786440 | tf_op jit(solution)/shard_map/ppermute | solution.py:19
  150.3 14.3 %collective-permute-start.3 = (bf16[2,256,256]{2,1,0:T(8,128)(2,1)}, bf16[2,256,256]{2,1,0:T(8,128)(2,1)S(1)}, u32[]{:S(2)}, u32[]{:S(2)}) collective-permute-start(bf16[2,256,256]{2,1,0:T(8,128)(2,1)} %collective-permute-done.2), channel_id=1, source_target_pairs={{0,4},{4,8},{8,12},{1,5},{5,9},{9,13},{2,6},{6,10},{10,14},{3,7},{... | collective-permute-start | bytes 786440 | tf_op jit(solution)/shard_map/ppermute | solution.py:19
  176.3 113.7 %all-gather.15.cloned.1.call-start = ((), (), s32[]{:S(2)}) async-start(), calls=%async_computation.8 | async-start | bytes 1310720 | tf_op jit(solution)/shard_map/all_gather | solution.py:117
  188.7 36.2 %copy-start.37 = (f32[128]{0:T(128)S(1)}, f32[128]{0:T(128)}, u32[]{:S(2)}) copy-start(f32[128]{0:T(128)} %param.14) | copy-start | bytes 1540
  223.0 2.2 copy-start.20
  223.0 2.2 copy-start.22
  224.3 24.8 %copy-start.3 = (f32[256,4,128]{2,1,0:T(4,128)}, f32[256,4,128]{2,1,0:T(4,128)S(1)}, u32[]{:S(2)}) copy-start(f32[256,4,128]{2,1,0:T(4,128)S(1)} %reshape.224) | copy-start | bytes 1572868
  224.3 24.8 %copy-start.6 = (bf16[1280,2,128]{2,1,0:T(2,128)(2,1)S(1)}, bf16[1280,2,128]{2,1,0:T(2,128)(2,1)}, u32[]{:S(2)}) copy-start(bf16[1280,2,128]{2,1,0:T(2,128)(2,1)} %reshape_squeeze.9) | copy-start | bytes 1966084
  224.9 24.2 %copy-start.27 = (f32[256,4]{1,0:T(8,128)}, f32[256,4]{1,0:T(8,128)S(1)}, u32[]{:S(2)}) copy-start(f32[256,4]{1,0:T(8,128)S(1)} %copy.90) | copy-start | bytes 12292
  249.1 3.2 copy-start.17
  249.1 3.2 copy-start.14
  249.1 3.2 copy-start.34
  263.3 127.7 %reduce-scatter.11.cloned.1.call-start = ((), (), s32[]{:S(2)}) async-start(), calls=%async_computation.12 | async-start | bytes 6881280 | tf_op jit(solution)/shard_map/reduce_scatter | solution.py:136
  295.3 174.0 %reduce-scatter.13.cloned.1.call-start = ((), (), s32[]{:S(2)}) async-start(), calls=%async_computation.13 | async-start | bytes 13762560
  306.0 5.7 %copy-start.15 = (bf16[1280,2,128,1]{0,2,3,1:T(8,128)(2,1)S(1)}, bf16[1280,2,128,1]{0,2,3,1:T(8,128)(2,1)}, u32[]{:S(2)}) copy-start(bf16[1280,2,128,1]{0,2,3,1:T(8,128)(2,1)} %copy.117) | copy-start | bytes 1966084
  306.0 3.6 collective-permute-start.4
  310.4 7.1 %collective-permute-start.5 = (bf16[2,256,256]{1,2,0:T(8,128)(2,1)}, bf16[2,256,256]{1,2,0:T(8,128)(2,1)}, u32[]{:S(2)}, u32[]{:S(2)}) collective-permute-start(bf16[2,256,256]{1,2,0:T(8,128)(2,1)} %fusion.29), channel_id=1, source_target_pairs={{4,0},{8,4},{12,8},{5,1},{9,5},{13,9},{6,2},{10,6},{14,10},{7,3},{... | collective-permute-start | bytes 786440 | tf_op jit(solution)/shard_map/ppermute | solution.py:19
  312.2 8.3 %copy-start.23 = (f32[256,64]{1,0:T(8,128)S(1)}, f32[256,64]{1,0:T(8,128)}, u32[]{:S(2)}) copy-start(f32[256,64]{1,0:T(8,128)} %copy-done.21) | copy-start | bytes 196612
  314.2 6.2 %copy-start.24 = (f32[256,4,64]{2,1,0:T(4,128)S(1)}, f32[256,4,64]{2,1,0:T(4,128)}, u32[]{:S(2)}) copy-start(f32[256,4,64]{2,1,0:T(4,128)} %copy.136) | copy-start | bytes 786436
  314.2 6.2 %copy-start.25 = (f32[256,4,64]{2,1,0:T(4,128)S(1)}, f32[256,4,64]{2,1,0:T(4,128)}, u32[]{:S(2)}) copy-start(f32[256,4,64]{2,1,0:T(4,128)} %copy.135) | copy-start | bytes 786436
  314.2 7.5 %copy-start.4 = (f32[256,4,128]{2,1,0:T(4,128)S(1)}, f32[256,4,128]{2,1,0:T(4,128)}, u32[]{:S(2)}) copy-start(f32[256,4,128]{2,1,0:T(4,128)} %copy-done.3) | copy-start | bytes 1572868
  319.1 13.9 %collective-permute-start.6 = (bf16[2,256,256]{1,2,0:T(8,128)(2,1)}, bf16[2,256,256]{1,2,0:T(8,128)(2,1)}, u32[]{:S(2)}, u32[]{:S(2)}) collective-permute-start(bf16[2,256,256]{1,2,0:T(8,128)(2,1)} %fusion.32), channel_id=1, source_target_pairs={{4,0},{8,4},{12,8},{5,1},{9,5},{13,9},{6,2},{10,6},{14,10},{7,3},{... | collective-permute-start | bytes 786440 | tf_op jit(solution)/shard_map/ppermute | solution.py:19
  320.8 15.4 %copy-start.28 = (f32[256,4]{1,0:T(8,128)S(1)}, f32[256,4]{1,0:T(8,128)}, u32[]{:S(2)}) copy-start(f32[256,4]{1,0:T(8,128)} %copy-done.27) | copy-start | bytes 12292
  334.7 13.9 %collective-permute-start.7 = (bf16[2,256,256]{1,2,0:T(8,128)(2,1)}, bf16[2,256,256]{1,2,0:T(8,128)(2,1)}, u32[]{:S(2)}, u32[]{:S(2)}) collective-permute-start(bf16[2,256,256]{1,2,0:T(8,128)(2,1)} %fusion.24), channel_id=1, source_target_pairs={{4,0},{8,4},{12,8},{5,1},{9,5},{13,9},{6,2},{10,6},{14,10},{7,3},{... | collective-permute-start | bytes 786440 | tf_op jit(solution)/shard_map/ppermute | solution.py:19
  338.2 11.4 %copy-start.9 = (bf16[256,4,128]{2,1,0:T(4,128)(2,1)}, bf16[256,4,128]{2,1,0:T(4,128)(2,1)S(1)}, u32[]{:S(2)}) copy-start(bf16[256,4,128]{2,1,0:T(4,128)(2,1)S(1)} %fusion.21) | copy-start | bytes 786436
  338.2 11.6 %copy-start.32 = (f32[256,64]{0,1:T(8,128)S(1)}, f32[256,64]{0,1:T(8,128)}, u32[]{:S(2)}) copy-start(f32[256,64]{0,1:T(8,128)} %copy.86) | copy-start | bytes 196612
  349.6 10.2 %copy-start.12 = (f32[2,256,256]{1,2,0:T(8,128)}, f32[2,256,256]{1,2,0:T(8,128)S(1)}, u32[]{:S(2)}) copy-start(f32[2,256,256]{1,2,0:T(8,128)S(1)} %fusion.33) | copy-start | bytes 1572868
  349.6 2.5 copy-start.30
  374.6 151.6 %reduce-scatter.9.cloned.1.call-start = ((), (), s32[]{:S(2)}) async-start(), calls=%async_computation.11 | async-start | bytes 3440640 | tf_op jit(solution)/shard_map/reduce_scatter | solution.py:202
  375.5 4.4 copy-start.5
  379.9 1.8 copy-start.11
  379.9 1.9 copy-start.13
  384.3 1.2 copy-start.26
  483.4 42.8 %copy-start.1 = (bf16[256,1344]{0,1:T(8,128)(2,1)S(1)}, bf16[256,1344]{0,1:T(8,128)(2,1)}, u32[]{:S(2)}) copy-start(bf16[256,1344]{0,1:T(8,128)(2,1)} %param.17) | copy-start | bytes 2064388
  (9 other events, 7.4 us)
Sparse Core Ops, SparseCore 0:
  9.6 59.6 all-gather.6
  70.9 25.0 all-gather.8
  97.5 26.3 all-gather.10
  125.3 45.5 all-gather.16
  172.3 45.6 all-gather.12
  220.8 27.1 reduce-scatter.6
  263.4 26.5 all-gather.14
  295.4 59.1 reduce-scatter.10
  374.7 94.5 reduce-scatter.12
  472.1 54.1 reduce-scatter.8
where the time goes:
time: 535 us; the launch traced here: 533 us
  waiting for transfers between devices  328 us (61%)
  local copies, waits for them, and re-layouts  63.6 us (12%)
  matrix products  63.2 us (12%)
  starting transfers between devices  38.1 us (7%)
  other arithmetic  25.4 us (5%)
  between operations  14.9 us (3%)
    unnamed x11, waiting for transfers between devices  77.9 us
    all_gather x1, waiting for transfers between devices, local(): full_rows = lax.all_gather(tokens, 'hid', axis=1, tiled=True)  57.2 us
    unnamed x90, local copies, waits for them, and re-layouts  41.8 us
    reduce_scatter x1, waiting for transfers between devices, local(): lax.psum_scatter(block_rows.astype(jnp.bfloat16), 'hid', scatter_dimensio...  38.4 us
    ppermute x8, starting transfers between devices, from_behind(): lax.ppermute(value, axis, [(source, source + steps) for source in range(f...  37 us
    all_gather x1, waiting for transfers between devices, local(): lax.all_gather(w_query, 'tok', axis=0, tiled=True)  29.4 us
    ppermute x8, waiting for transfers between devices, from_behind(): lax.ppermute(value, axis, [(source, source + steps) for source in range(f...  28.1 us
    all_gather x1, waiting for transfers between devices, local(): all_heads = lax.all_gather(attended, 'hid', axis=1, tiled=True)  26.7 us
  transfers between devices with their start and end apart: 18, of which 16 were waited for; matrix products, arithmetic and copies ran while one was open for 24% of the time, Pallas kernels for 0%

commit v1 on v0

--- a/solution.py
+++ b/solution.py
@@ -11,6 +11,28 @@
 attn_scale = 168.0 ** (-0.5)
 rope_base = 10000.0
 norm_eps = 1e-06
+
+
+def laid_out(parts, dim):
+    parts = jnp.moveaxis(parts, 0, dim)
+    shape = parts.shape
+    return parts.reshape(*shape[:dim], shape[dim] * shape[dim + 1], *shape[dim + 2 :])
+
+
+def doubled(x, axis):
+    size = lax.axis_size(axis)
+    parts = x[None]
+    for level in range(size.bit_length() - 1):
+        bit = 1 << level
+        theirs = lax.ppermute(parts, axis, [(i, i ^ bit) for i in range(size)])
+        both = jnp.stack([parts, theirs])
+        upper = lax.axis_index(axis) >> level & 1
+        parts = jnp.where(upper == 0, both, both[::-1]).reshape(-1, *x.shape)
+    return parts
+
+
+def doubled_up(array, axis, dim):
+    return laid_out(doubled(array, axis), dim)
 
 
 def from_behind(value, axis, steps):
@@ -64,7 +86,7 @@
     pieces = (
         lax.all_gather(w_query, "tok", axis=0, tiled=True),
         lax.all_gather(key_weight, "tok", axis=0, tiled=True),
-        lax.all_gather(value_weight, "tok", axis=0, tiled=True),
+        doubled_up(value_weight, "tok", 0),
     )
     columns = full_rows
     query_unnormed = jnp.dot(columns, pieces[0], preferred_element_type=jnp.float32)

time: 535 us -> 507 us (0.948)
  waiting for transfers between devices: 328 us -> 280 us
  starting transfers between devices: 38.1 us -> 45.8 us
  other arithmetic: 25.4 us -> 31.7 us
  matrix products: 63.2 us -> 69.4 us
    all_gather x1, waiting for transfers between devices: 57.2 us -> 18 us  [local(): full_rows = lax.all_gather(tokens, 'hid', axis=1, tiled=True)]
    ppermute x0 -> x2, waiting for transfers between devices: none -> 31.1 us  [doubled(): theirs = lax.ppermute(parts, axis, [(i, i ^ bit) for i in range(size)])]
    all_gather x1, waiting for transfers between devices: 20.9 us -> 0.01 us  [local(): lax.all_gather(value_weight, 'tok', axis=0, tiled=True)]
    all_gather x1, waiting for transfers between devices: 29.4 us -> 18.4 us  [local(): lax.all_gather(w_query, 'tok', axis=0, tiled=True)]
    ppermute x8, waiting for transfers between devices: 28.1 us -> 21.8 us  [from_behind(): lax.ppermute(value, axis, [(source, source + steps) for source in range(f...]
  transfers between devices with their start and end apart: 18 -> 20, of which waited for: 16 -> 16; matrix products, arithmetic and copies ran while one was open for 24% -> 28% of each run, Pallas kernels for 0% -> 0%
where the time goes in v1:
time: 507 us; the launch traced here: 505 us
  waiting for transfers between devices  280 us (55%)
  matrix products  69.4 us (14%)
  local copies, waits for them, and re-layouts  62.6 us (12%)
  starting transfers between devices  45.8 us (9%)
  other arithmetic  31.7 us (6%)
  between operations  14.9 us (3%)
    unnamed x11, waiting for transfers between devices  78.1 us
    ppermute x8, starting transfers between devices, from_behind(): lax.ppermute(value, axis, [(source, source + steps) for source in range(f...  41.4 us
    unnamed x90, local copies, waits for them, and re-layouts  40.8 us
    reduce_scatter x1, waiting for transfers between devices, local(): lax.psum_scatter(block_rows.astype(jnp.bfloat16), 'hid', scatter_dimensio...  38.4 us
    ppermute x2, waiting for transfers between devices, doubled(): theirs = lax.ppermute(parts, axis, [(i, i ^ bit) for i in range(size)])  31.1 us
    all_gather x1, waiting for transfers between devices, local(): lax.all_gather(key_weight, 'tok', axis=0, tiled=True)  26.6 us
    all_gather x1, waiting for transfers between devices, local(): all_heads = lax.all_gather(attended, 'hid', axis=1, tiled=True)  25.9 us
    reduce_scatter x1, waiting for transfers between devices, local(): lax.psum_scatter(partial_heads.astype(jnp.bfloat16), 'hid', scatter_dimen...  22.1 us
  transfers between devices with their start and end apart: 20, of which 16 were waited for; matrix products, arithmetic and copies ran while one was open for 28% of the time, Pallas kernels for 0%

profile of v1, /device:TPU:0, one launch (start us, length us, event | category | flops | bytes accessed | tf_op | source)
XLA Modules:
  0.0 504.8 jit_solution(6852873090450270514)
XLA Ops:
  10.6 1.8 collective-permute-done
  13.9 2.9 collective-permute-start.1
  18.2 29.4 %collective-permute-done.1 = bf16[2,1344,256]{2,1,0:T(8,128)(2,1)} collective-permute-done((bf16[2,1344,256]{2,1,0:T(8,128)(2,1)}, bf16[2,1344,256]{2,1,0:T(8,128)(2,1)}, u32[]{:S(2)}, u32[]{:S(2)}) %collective-permute-start.1) | collective-permute-done | bytes 1376288 | tf_op jit(solution)/shard_map/ppermute | solution.py:27
  49.2 2.1 reverse_select_fusion
  51.3 18.0 %all-gather.7.cloned.1.call-done = bf16[256,5376]{0,1:T(8,128)(2,1)} async-done(((bf16[256,1344]{0,1:T(8,128)(2,1)}), bf16[256,5376]{0,1:T(8,128)(2,1)}) %all-gather.7.cloned.1.call-update) | async-done | bytes 2752528 | tf_op jit(solution)/shard_map/all_gather | solution.py:85
  69.3 26.6 %all-gather.9.cloned.1.call-done = bf16[5376,256]{1,0:T(8,128)(2,1)} async-done(((bf16[1344,256]{1,0:T(8,128)(2,1)}), bf16[5376,256]{1,0:T(8,128)(2,1)}) %all-gather.9.cloned.1.call-update) | async-done | bytes 2752528 | tf_op jit(solution)/shard_map/all_gather | solution.py:88
  95.9 3.8 multiply_reduce_fusion.3
  103.0 3.3 fusion.17
  106.9 2.1 collective-permute-start.2
  110.9 10.3 %collective-permute-start.3 = (bf16[2,256,256]{2,1,0:T(8,128)(2,1)S(1)}, bf16[2,256,256]{2,1,0:T(8,128)(2,1)}, u32[]{:S(2)}, u32[]{:S(2)}) collective-permute-start(bf16[2,256,256]{2,1,0:T(8,128)(2,1)S(1)} %collective-permute-done.2), channel_id=1, source_target_pairs={{0,4},{4,8},{8,12},{1,5},{5,9},{9,13},{2,6},{6,10},{10,14},{3,7},{... | collective-permute-start | bytes 786440 | tf_op jit(solution)/shard_map/ppermute | solution.py:41
  121.8 12.7 %collective-permute-start.4 = (bf16[2,256,256]{2,1,0:T(8,128)(2,1)}, bf16[2,256,256]{2,1,0:T(8,128)(2,1)}, u32[]{:S(2)}, u32[]{:S(2)}) collective-permute-start(bf16[2,256,256]{2,1,0:T(8,128)(2,1)} %collective-permute-done.3), channel_id=1, source_target_pairs={{0,4},{4,8},{8,12},{1,5},{5,9},{9,13},{2,6},{6,10},{10,14},{3,7},{... | collective-permute-start | bytes 786440 | tf_op jit(solution)/shard_map/ppermute | solution.py:41
  135.3 10.9 %collective-permute-start.5 = (bf16[2,256,256]{2,1,0:T(8,128)(2,1)}, bf16[2,256,256]{2,1,0:T(8,128)(2,1)S(1)}, u32[]{:S(2)}, u32[]{:S(2)}) collective-permute-start(bf16[2,256,256]{2,1,0:T(8,128)(2,1)} %collective-permute-done.4), channel_id=1, source_target_pairs={{0,4},{4,8},{8,12},{1,5},{5,9},{9,13},{2,6},{6,10},{10,14},{3,7},{... | collective-permute-start | bytes 786440 | tf_op jit(solution)/shard_map/ppermute | solution.py:41
  146.2 2.1 fusion.11
  154.0 6.0 %convolution_convert_fusion.3 = bf16[256,2048]{1,0:T(8,128)(2,1)} fusion(bf16[256,1344]{0,1:T(8,128)(2,1)S(1)} %copy-done, bf16[2048,1344]{0,1:T(8,128)(2,1)} %all-gather.15.cloned.1.call-done), kind=kOutput, calls=%fused_computation.25 | convolution fusion | flops 1409810432 | bytes 7241728 | tf_op jit(solution)/shard_map/td,hd->th/dot_general | solution.py:147
  161.9 2.4 fusion.52
  164.4 2.5 reshape_squeeze.9
  166.9 2.5 reshape_squeeze.10
  169.4 2.9 copy.117
  172.3 18.4 %all-gather.11.cloned.1.call-done = bf16[5376,512]{1,0:T(8,128)(2,1)} async-done(((bf16[1344,512]{1,0:T(8,128)(2,1)}), bf16[5376,512]{1,0:T(8,128)(2,1)}) %all-gather.11.cloned.1.call-update) | async-done | bytes 5505040 | tf_op jit(solution)/shard_map/all_gather | solution.py:87
  190.8 5.0 fusion.55
  198.6 22.1 %reduce-scatter.7.cloned.1.call-done = bf16[256,512]{1,0:T(8,128)(2,1)} async-done(((bf16[256,2048]{1,0:T(8,128)(2,1)}), bf16[256,512]{1,0:T(8,128)(2,1)}) %reduce-scatter.7.cloned.1.call-update) | async-done | bytes 262160 | tf_op jit(solution)/shard_map/reduce_scatter | solution.py:153
  221.8 3.2 fusion.21
  225.0 7.2 %fusion.2 = (f32[2,2,256]{2,1,0:T(2,128)S(1)}, f32[2,2,256,1280]{2,3,1,0:T(8,128)}) fusion(f32[2,1280,256,2]{2,1,3,0:T(8,128)} %fusion.21, bf16[1280,2,128,1]{0,2,3,1:T(8,128)(2,1)S(1)} %copy-done.14, pred[256,1280]{0,1:T(8,128)(4,1)S(1)} %copy-done.34, bf16[256,2,2,64]{3,0,2,1:T(8,128)(2,1)S(1)} %bitcast.117, bf16[256,2,2,64]{3,0,2,1:T(8,128)(2,1)S(1)} %bitcast.119), kind=kOutput, calls=%fused_computation.8 | convolution fusion | flops 342623488 | bytes 11735040 | tf_op jit(solution)/shard_map/div | solution.py:133
  232.2 3.8 fusion.14
  236.8 25.9 %all-gather.13.cloned.1.call-done = bf16[256,2048]{0,1:T(8,128)(2,1)} async-done(((bf16[256,512]{0,1:T(8,128)(2,1)}), bf16[256,2048]{0,1:T(8,128)(2,1)}) %all-gather.13.cloned.1.call-update) | async-done | bytes 1048592 | tf_op jit(solution)/shard_map/all_gather | solution.py:139
  262.7 5.3 %convolution_convert_fusion.1 = bf16[2048,1344]{0,1:T(8,128)(2,1)} fusion(bf16[256,2048]{0,1:T(8,128)(2,1)} %all-gather.13.cloned.1.call-done, bf16[256,1344]{0,1:T(8,128)(2,1)S(1)} %copy-done), kind=kOutput, calls=%fused_computation.5 | convolution fusion | flops 1412038656 | bytes 7241728 | tf_op jit(solution)/shard_map/th,td->hd/dot_general | solution.py:159
  268.2 5.7 %fusion.4 = bf16[2,2,256,1280]{2,3,1,0:T(8,128)(2,1)S(1)} fusion(f32[2,1280,256,2]{2,1,3,0:T(8,128)} %fusion.21, f32[2,2,256,1280]{2,3,1,0:T(8,128)} %get-tuple-element.53, f32[2,2,256]{2,1,0:T(2,128)S(1)} %get-tuple-element.52), kind=kLoop, calls=%fused_computation.10 | loop fusion | flops 5242880 | bytes 13111296 | tf_op jit(solution)/shard_map/convert_element_type | solution.py:174
  275.0 3.5 fusion.7
  280.0 2.1 collective-permute-done.6
  286.8 8.9 %collective-permute-done.7 = bf16[2,256,256]{1,2,0:T(8,128)(2,1)} collective-permute-done((bf16[2,256,256]{1,2,0:T(8,128)(2,1)}, bf16[2,256,256]{1,2,0:T(8,128)(2,1)}, u32[]{:S(2)}, u32[]{:S(2)}) %collective-permute-start.7) | collective-permute-done | bytes 262176 | tf_op jit(solution)/shard_map/ppermute | solution.py:41
  300.7 5.0 collective-permute-done.8
  305.7 1.7 fusion.26
  308.9 2.0 fusion.23
  311.7 3.4 collective-permute-done.9
  318.8 7.7 %fusion = bf16[5376,1024]{0,1:T(8,128)(2,1)} fusion(bf16[256,5376]{0,1:T(8,128)(2,1)} %all-gather.7.cloned.1.call-done, bf16[256,256]{1,0:T(8,128)(2,1)S(1)} %copy.109, bf16[256,256]{1,0:T(8,128)(2,1)S(1)} %copy.108, bf16[256,512]{1,0:T(8,128)(2,1)S(1)} %bitcast.116), kind=kOutput, calls=%fused_computation.1 | convolution fusion | flops 2825650176 | bytes 14286848 | tf_op jit(solution)/shard_map/td,tc->dc/dot_general | solution.py:230
  326.5 14.7 %copy.133 = bf16[5376,1024]{1,0:T(8,128)(2,1)} copy(bf16[5376,1024]{0,1:T(8,128)(2,1)} %fusion) | data formatting | bytes 22020096
  342.2 4.5 fusion.49
  346.7 3.2 convolution_add_fusion.1
  349.9 5.9 %fusion.1 = bf16[256,5376]{0,1:T(8,128)(2,1)} fusion(f32[256,5376]{0,1:T(8,128)} %convolution_add_fusion.1, bf16[5376,256]{1,0:T(8,128)(2,1)} %all-gather.17.cloned.1.call-done, f32[2,256,256]{1,2,0:T(8,128)S(1)} %copy-done.13), kind=kOutput, calls=%fused_computation.4 | convolution fusion | flops 707395584 | bytes 11141120 | tf_op jit(solution)/shard_map/tc,dc->td/dot_general | solution.py:221
  357.1 5.6 %convolution_convert_fusion.2 = bf16[256,1344]{0,1:T(8,128)(2,1)} fusion(bf16[2048,1344]{0,1:T(8,128)(2,1)} %all-gather.15.cloned.1.call-done, bf16[256,2048]{0,1:T(8,128)(2,1)S(1)} %copy-done.26), kind=kOutput, calls=%fused_computation.24 | convolution fusion | flops 1409630208 | bytes 7241728 | tf_op jit(solution)/shard_map/dot_general | solution.py:141
  362.7 3.6 convert_element_type.115
  366.4 74.7 %reduce-scatter.13.cloned.1.call-done = bf16[1344,1024]{1,0:T(8,128)(2,1)} async-done(((bf16[5376,1024]{1,0:T(8,128)(2,1)}), bf16[1344,1024]{1,0:T(8,128)(2,1)}) %reduce-scatter.13.cloned.1.call-update) | async-done | bytes 2752528
  441.1 4.6 copy.134
  445.6 3.1 slice.82
  448.8 3.8 copy.110
  452.5 2.6 fusion.51
  455.2 2.9 copy.111
  459.6 38.4 %reduce-scatter.9.cloned.1.call-done = bf16[256,1344]{0,1:T(8,128)(2,1)} async-done(((bf16[256,5376]{0,1:T(8,128)(2,1)}), bf16[256,1344]{0,1:T(8,128)(2,1)}) %reduce-scatter.9.cloned.1.call-update) | async-done | bytes 688144 | tf_op jit(solution)/shard_map/reduce_scatter | solution.py:224
  (165 shorter events, 49.0 us)
Async XLA Ops:
  7.2 146.9 %copy-start = (bf16[256,1344]{0,1:T(8,128)(2,1)S(1)}, bf16[256,1344]{0,1:T(8,128)(2,1)}, u32[]{:S(2)}) copy-start(bf16[256,1344]{0,1:T(8,128)(2,1)} %param.17) | copy-start | bytes 2064388
  7.2 2.9 copy-start.11
  7.2 62.1 %all-gather.7.cloned.1.call-start = ((), (), s32[]{:S(2)}) async-start(), calls=%async_computation.4 | async-start | bytes 3440640 | tf_op jit(solution)/shard_map/all_gather | solution.py:85
  7.9 88.0 %all-gather.9.cloned.1.call-start = ((), (), s32[]{:S(2)}) async-start(), calls=%async_computation.5 | async-start | bytes 3440640 | tf_op jit(solution)/shard_map/all_gather | solution.py:88
  8.7 145.3 %all-gather.15.cloned.1.call-start = ((), (), s32[]{:S(2)}) async-start(), calls=%async_computation.8 | async-start | bytes 6881280 | tf_op jit(solution)/shard_map/all_gather | solution.py:143
  9.4 181.3 %all-gather.11.cloned.1.call-start = ((), (), s32[]{:S(2)}) async-start(), calls=%async_computation.6 | async-start | bytes 6881280 | tf_op jit(solution)/shard_map/all_gather | solution.py:87
  10.0 210.7 %reduce-scatter.7.cloned.1.call-start = ((), (), s32[]{:S(2)}) async-start(), calls=%async_computation.9 | async-start | bytes 1310720 | tf_op jit(solution)/shard_map/reduce_scatter | solution.py:153
  10.0 2.3 collective-permute-start
  12.5 4.3 copy-start.36
  13.9 33.7 %collective-permute-start.1 = (bf16[2,1344,256]{2,1,0:T(8,128)(2,1)}, bf16[2,1344,256]{2,1,0:T(8,128)(2,1)}, u32[]{:S(2)}, u32[]{:S(2)}) collective-permute-start(bf16[2,1344,256]{2,1,0:T(8,128)(2,1)} %get-tuple-element.35), channel_id=1, source_target_pairs={{0,8},{4,12},{8,0},{12,4},{1,9},{5,13},{9,1},{13,5},{2,10},{6,14},... | collective-permute-start | bytes 4128776 | tf_op jit(solution)/shard_map/ppermute | solution.py:27
  17.4 31.8 %copy-start.19 = (f32[256,64]{1,0:T(8,128)}, f32[256,64]{1,0:T(8,128)S(1)}, u32[]{:S(2)}) copy-start(f32[256,64]{1,0:T(8,128)S(1)} %get-tuple-element.48) | copy-start | bytes 196612
  17.4 31.8 %copy-start.21 = (f32[256,64]{1,0:T(8,128)}, f32[256,64]{1,0:T(8,128)S(1)}, u32[]{:S(2)}) copy-start(f32[256,64]{1,0:T(8,128)S(1)} %get-tuple-element.49) | copy-start | bytes 196612
  51.3 49.2 %copy-start.38 = (f32[128]{0:T(128)S(1)}, f32[128]{0:T(128)}, u32[]{:S(2)}) copy-start(f32[128]{0:T(128)} %param.15) | copy-start | bytes 1540
  69.3 33.6 %copy-start.2 = (bf16[256,5376]{0,1:T(8,128)(2,1)S(1)}, bf16[256,5376]{0,1:T(8,128)(2,1)}, u32[]{:S(2)}) copy-start(bf16[256,5376]{0,1:T(8,128)(2,1)} %all-gather.7.cloned.1.call-done) | copy-start | bytes 8257540
  95.9 4.6 copy-start.31
  103.0 3.3 copy-start.29
  106.9 3.3 collective-permute-start.2
  110.9 10.9 %collective-permute-start.3 = (bf16[2,256,256]{2,1,0:T(8,128)(2,1)S(1)}, bf16[2,256,256]{2,1,0:T(8,128)(2,1)}, u32[]{:S(2)}, u32[]{:S(2)}) collective-permute-start(bf16[2,256,256]{2,1,0:T(8,128)(2,1)S(1)} %collective-permute-done.2), channel_id=1, source_target_pairs={{0,4},{4,8},{8,12},{1,5},{5,9},{9,13},{2,6},{6,10},{10,14},{3,7},{... | collective-permute-start | bytes 786440 | tf_op jit(solution)/shard_map/ppermute | solution.py:41
  121.8 13.5 %collective-permute-start.4 = (bf16[2,256,256]{2,1,0:T(8,128)(2,1)}, bf16[2,256,256]{2,1,0:T(8,128)(2,1)}, u32[]{:S(2)}, u32[]{:S(2)}) collective-permute-start(bf16[2,256,256]{2,1,0:T(8,128)(2,1)} %collective-permute-done.3), channel_id=1, source_target_pairs={{0,4},{4,8},{8,12},{1,5},{5,9},{9,13},{2,6},{6,10},{10,14},{3,7},{... | collective-permute-start | bytes 786440 | tf_op jit(solution)/shard_map/ppermute | solution.py:41
  135.3 13.0 %collective-permute-start.5 = (bf16[2,256,256]{2,1,0:T(8,128)(2,1)}, bf16[2,256,256]{2,1,0:T(8,128)(2,1)S(1)}, u32[]{:S(2)}, u32[]{:S(2)}) collective-permute-start(bf16[2,256,256]{2,1,0:T(8,128)(2,1)} %collective-permute-done.4), channel_id=1, source_target_pairs={{0,4},{4,8},{8,12},{1,5},{5,9},{9,13},{2,6},{6,10},{10,14},{3,7},{... | collective-permute-start | bytes 786440 | tf_op jit(solution)/shard_map/ppermute | solution.py:41
  160.0 102.7 %all-gather.13.cloned.1.call-start = ((), (), s32[]{:S(2)}) async-start(), calls=%async_computation.7 | async-start | bytes 1310720 | tf_op jit(solution)/shard_map/all_gather | solution.py:139
  172.3 25.3 %copy-start.37 = (f32[128]{0:T(128)S(1)}, f32[128]{0:T(128)}, u32[]{:S(2)}) copy-start(f32[128]{0:T(128)} %param.14) | copy-start | bytes 1540
  197.0 24.8 %copy-start.3 = (f32[256,4,128]{2,1,0:T(4,128)}, f32[256,4,128]{2,1,0:T(4,128)S(1)}, u32[]{:S(2)}) copy-start(f32[256,4,128]{2,1,0:T(4,128)S(1)} %reshape.228) | copy-start | bytes 1572868
  197.0 24.8 %copy-start.6 = (bf16[1280,2,128]{2,1,0:T(2,128)(2,1)S(1)}, bf16[1280,2,128]{2,1,0:T(2,128)(2,1)}, u32[]{:S(2)}) copy-start(bf16[1280,2,128]{2,1,0:T(2,128)(2,1)} %reshape_squeeze.9) | copy-start | bytes 1966084
  197.6 24.2 %copy-start.27 = (f32[256,4]{1,0:T(8,128)}, f32[256,4]{1,0:T(8,128)S(1)}, u32[]{:S(2)}) copy-start(f32[256,4]{1,0:T(8,128)S(1)} %copy.90) | copy-start | bytes 12292
  221.7 3.2 copy-start.17
  221.8 3.2 copy-start.14
  221.8 3.2 copy-start.34
  236.0 113.9 %all-gather.17.cloned.1.call-start = ((), (), s32[]{:S(2)}) async-start(), calls=%async_computation.10 | async-start | bytes 3440640 | tf_op jit(solution)/shard_map/all_gather | solution.py:215
  236.7 126.0 %reduce-scatter.11.cloned.1.call-start = ((), (), s32[]{:S(2)}) async-start(), calls=%async_computation.12 | async-start | bytes 6881280 | tf_op jit(solution)/shard_map/reduce_scatter | solution.py:158
  268.0 173.1 %reduce-scatter.13.cloned.1.call-start = ((), (), s32[]{:S(2)}) async-start(), calls=%async_computation.13 | async-start | bytes 13762560
  278.5 5.7 %copy-start.15 = (bf16[1280,2,128,1]{0,2,3,1:T(8,128)(2,1)S(1)}, bf16[1280,2,128,1]{0,2,3,1:T(8,128)(2,1)}, u32[]{:S(2)}) copy-start(bf16[1280,2,128,1]{0,2,3,1:T(8,128)(2,1)} %copy.117) | copy-start | bytes 1966084
  278.6 3.6 collective-permute-start.6
  282.9 12.7 %collective-permute-start.7 = (bf16[2,256,256]{1,2,0:T(8,128)(2,1)}, bf16[2,256,256]{1,2,0:T(8,128)(2,1)}, u32[]{:S(2)}, u32[]{:S(2)}) collective-permute-start(bf16[2,256,256]{1,2,0:T(8,128)(2,1)} %fusion.31), channel_id=1, source_target_pairs={{4,0},{8,4},{12,8},{5,1},{9,5},{13,9},{6,2},{10,6},{14,10},{7,3},{... | collective-permute-start | bytes 786440 | tf_op jit(solution)/shard_map/ppermute | solution.py:41
  284.7 13.9 %copy-start.23 = (f32[256,64]{1,0:T(8,128)S(1)}, f32[256,64]{1,0:T(8,128)}, u32[]{:S(2)}) copy-start(f32[256,64]{1,0:T(8,128)} %copy-done.21) | copy-start | bytes 196612
  286.8 11.9 %copy-start.24 = (f32[256,4,64]{2,1,0:T(4,128)S(1)}, f32[256,4,64]{2,1,0:T(4,128)}, u32[]{:S(2)}) copy-start(f32[256,4,64]{2,1,0:T(4,128)} %copy.136) | copy-start | bytes 786436
  286.8 11.9 %copy-start.25 = (f32[256,4,64]{2,1,0:T(4,128)S(1)}, f32[256,4,64]{2,1,0:T(4,128)}, u32[]{:S(2)}) copy-start(f32[256,4,64]{2,1,0:T(4,128)} %copy.135) | copy-start | bytes 786436
  286.8 13.2 %copy-start.4 = (f32[256,4,128]{2,1,0:T(4,128)S(1)}, f32[256,4,128]{2,1,0:T(4,128)}, u32[]{:S(2)}) copy-start(f32[256,4,128]{2,1,0:T(4,128)} %copy-done.3) | copy-start | bytes 1572868
  297.4 8.4 %collective-permute-start.8 = (bf16[2,256,256]{1,2,0:T(8,128)(2,1)}, bf16[2,256,256]{1,2,0:T(8,128)(2,1)}, u32[]{:S(2)}, u32[]{:S(2)}) collective-permute-start(bf16[2,256,256]{1,2,0:T(8,128)(2,1)} %fusion.34), channel_id=1, source_target_pairs={{4,0},{8,4},{12,8},{5,1},{9,5},{13,9},{6,2},{10,6},{14,10},{7,3},{... | collective-permute-start | bytes 786440 | tf_op jit(solution)/shard_map/ppermute | solution.py:41
  299.0 9.9 %copy-start.28 = (f32[256,4]{1,0:T(8,128)S(1)}, f32[256,4]{1,0:T(8,128)}, u32[]{:S(2)}) copy-start(f32[256,4]{1,0:T(8,128)} %copy-done.27) | copy-start | bytes 12292
  307.5 7.6 %collective-permute-start.9 = (bf16[2,256,256]{1,2,0:T(8,128)(2,1)}, bf16[2,256,256]{1,2,0:T(8,128)(2,1)}, u32[]{:S(2)}, u32[]{:S(2)}) collective-permute-start(bf16[2,256,256]{1,2,0:T(8,128)(2,1)} %fusion.26), channel_id=1, source_target_pairs={{4,0},{8,4},{12,8},{5,1},{9,5},{13,9},{6,2},{10,6},{14,10},{7,3},{... | collective-permute-start | bytes 786440 | tf_op jit(solution)/shard_map/ppermute | solution.py:41
  310.9 5.2 %copy-start.9 = (bf16[256,4,128]{2,1,0:T(4,128)(2,1)}, bf16[256,4,128]{2,1,0:T(4,128)(2,1)S(1)}, u32[]{:S(2)}) copy-start(bf16[256,4,128]{2,1,0:T(4,128)(2,1)S(1)} %fusion.23) | copy-start | bytes 786436
  311.0 5.4 %copy-start.32 = (f32[256,64]{0,1:T(8,128)S(1)}, f32[256,64]{0,1:T(8,128)}, u32[]{:S(2)}) copy-start(f32[256,64]{0,1:T(8,128)} %copy.86) | copy-start | bytes 196612
  316.2 10.3 %copy-start.12 = (f32[2,256,256]{1,2,0:T(8,128)}, f32[2,256,256]{1,2,0:T(8,128)S(1)}, u32[]{:S(2)}) copy-start(f32[2,256,256]{1,2,0:T(8,128)S(1)} %fusion.35) | copy-start | bytes 1572868
  341.3 156.7 %reduce-scatter.9.cloned.1.call-start = ((), (), s32[]{:S(2)}) async-start(), calls=%async_computation.11 | async-start | bytes 3440640 | tf_op jit(solution)/shard_map/reduce_scatter | solution.py:224
  342.2 4.5 copy-start.5
  346.7 3.3 copy-start.13
  455.2 42.8 %copy-start.1 = (bf16[256,1344]{0,1:T(8,128)(2,1)S(1)}, bf16[256,1344]{0,1:T(8,128)(2,1)}, u32[]{:S(2)}) copy-start(bf16[256,1344]{0,1:T(8,128)(2,1)} %param.17) | copy-start | bytes 2064388
  (11 other events, 14.1 us)
Sparse Core Ops, SparseCore 0:
  9.6 59.6 all-gather.6
  70.9 25.0 all-gather.8
  97.5 46.0 all-gather.14
  145.0 45.7 all-gather.10
  193.5 27.1 reduce-scatter.6
  236.1 26.5 all-gather.12
  264.3 28.5 all-gather.16
  295.6 55.3 reduce-scatter.10
  353.6 87.4 reduce-scatter.12
  443.8 54.1 reduce-scatter.8
